TPU v7x, 256 devices: a whole 4x4x8 slice. The times are simulated.
256 devices in a mesh: row: 8 (over y_lo, x), col: 32 (over y_hi, z, core).
Axes of the slice: x: 4, y: 4 (y_hi: 2, y_lo: 2; y = y_hi * 2 + y_lo), z: 8, core: 2. Of those that a mesh axis runs over, the one named last changes fastest.
Arguments:
- queries: bfloat16 [24576, 1024], P(('row', 'col')), may hold values from -128 to 128
- keys: bfloat16 [24576, 128], P(('row', 'col')), may hold values from -4 to 4
- values: bfloat16 [24576, 128], P(('row', 'col')), may hold values from -6 to 6
- block_start: int32 [256], P(('row', 'col')), may hold values from 0 to 255, as said below
Outputs:
- attended: float32 [24576, 1024], P(('row', 'col'))
- log_total: float32 [24576, 8], P(('row', 'col'))
Inputs may be any that keep to these rules, and one draw needn't show every extreme that they name: `block_start`: a permutation of 0 to 255.
All inputs are finite; a program needn't handle non-finite values.
Results may differ from a plain program's by a relative error of at most 0.0028.
Values may be sent and summed in bfloat16 or wider, within the bound.
A program may use at most 64 MiB of HBM per device.

v0:
```python
import jax
import jax.numpy as jnp
from jax import lax
from jax.sharding import PartitionSpec as P


def pick_block(piece_len):
    limit = min(piece_len, 1024)
    for size in range(limit, 0, -1):
        if piece_len % size == 0:
            return size
    return piece_len


def local(queries, keys, values, block_start):
    tokens_here = queries.shape[0]
    head_width = keys.shape[1]
    heads_count = queries.shape[1] // head_width
    scale = head_width ** (-0.5)
    query_rows = queries.reshape(tokens_here * heads_count, head_width)
    query_pos = block_start[0] * tokens_here + jnp.arange(tokens_here, dtype=jnp.int32)
    row_pos = jnp.repeat(query_pos, heads_count)
    all_starts = lax.all_gather(block_start, ("row", "col"), axis=0, tiled=True)
    block_ids = jnp.arange(all_starts.shape[0], dtype=jnp.int32)
    paired = jnp.concatenate([keys, values], axis=1)

    def update(state_now, key_block, key_pos):
        accum, peak, total = state_now
        key_part = key_block[:, :head_width]
        value_part = key_block[:, head_width:]
        scores = (
            lax.dot_general(
                query_rows, key_part, (((1,), (1,)), ((), ())), preferred_element_type=jnp.float32
            )
            * scale
        )
        kept = key_pos[None, :] <= row_pos[:, None]
        scores = jnp.where(kept, scores, -1e30)
        new_peak = jnp.maximum(peak, jnp.max(scores, axis=1))
        rescale = jnp.exp(peak - new_peak)
        weights = jnp.where(kept, jnp.exp(scores - new_peak[:, None]), 0.0)
        total = total * rescale + jnp.sum(weights, axis=1)
        accum = accum * rescale[:, None] + jnp.dot(
            weights.astype(jnp.bfloat16), value_part, preferred_element_type=jnp.float32
        )
        return (accum, new_peak, total)

    rows_all = tokens_here * heads_count
    initial = (
        jnp.zeros((rows_all, head_width), jnp.float32),
        jnp.full((rows_all,), -1e30, jnp.float32),
        jnp.zeros((rows_all,), jnp.float32),
    )
    key_piece = lax.all_gather(paired, ("row", "col"), axis=0, tiled=True)
    piece_len = key_piece.shape[0]
    block_len = pick_block(piece_len)
    count = piece_len // block_len
    key_index = jnp.arange(piece_len, dtype=jnp.int32)
    owner = key_index // tokens_here
    lookup = jnp.sum(
        jnp.where(owner[:, None] == block_ids[None, :], all_starts[None, :], 0), axis=1
    )
    piece_pos = lookup * tokens_here + key_index % tokens_here

    def turn(index, state_in):
        key_block = lax.dynamic_slice_in_dim(key_piece, index * block_len, block_len, 0)
        key_pos = lax.dynamic_slice_in_dim(piece_pos, index * block_len, block_len, 0)
        state_out = update(state_in, key_block, key_pos)
        return state_out

    accum, peak, total = lax.fori_loop(0, count, turn, initial)
    attended = (accum / total[:, None]).reshape(tokens_here, heads_count * head_width)
    log_total = (peak + jnp.log(total)).reshape(tokens_here, heads_count)
    return (attended, log_total)


def solution(mesh):
    placed = (
        P(("row", "col"), None),
        P(("row", "col"), None),
        P(("row", "col"), None),
        P(("row", "col")),
    )
    return jax.shard_map(
        local,
        mesh=mesh,
        in_specs=placed,
        out_specs=(P(("row", "col"), None), P(("row", "col"), None)),
        check_vma=False,
    )
```

profile of v0, /device:TPU:1, one launch (start us, length us, event | category | flops | bytes accessed | tf_op | source)
XLA Modules:
  0.0 564.0 jit_solution(6795313790271823186)
XLA Ops:
  10.5 81.4 %all-reduce = s32[256]{0:T(256)S(1)} all-reduce(s32[256]{0:T(256)S(1)} %dynamic-update-slice), channel_id=1, replica_groups=mesh['row'=8,'col'=32] {'row','col'}, use_global_device_ids=true, to_apply=%add | all-reduce | flops 256 | bytes 2048
  91.9 14.9 %select_reduce_fusion = s32[24576]{0:T(1024)S(1)} fusion(s32[256]{0:T(256)S(1)} %all-reduce, s32[24576]{0:T(1024)S(1)} %add_select_fusion), kind=kLoop, calls=%fused_computation.20 | loop fusion | flops 18849792 | bytes 197632 | tf_op jit(solution)/shard_map/reduce_sum | solution.py:60
  106.9 332.2 %all-gather.2.cloned.1.call-done = bf16[24576,256]{1,0:T(8,128)(2,1)} async-done(((bf16[96,256]{1,0:T(8,128)(2,1)}), bf16[24576,256]{1,0:T(8,128)(2,1)}) %all-gather.2.cloned.1.call-update) | async-done | bytes 12582928 | tf_op jit(solution)/shard_map/all_gather | solution.py:54
  439.1 116.4 %while.18 = (s32[]{:T(128)}, f32[768,128]{1,0:T(8,128)S(1)}, f32[768]{0:T(1024)S(1)}, f32[768]{0:T(1024)S(1)}, s32[24576]{0:T(1024)S(1)}, /*index=5*/bf16[24576,...) while((s32[]{:T(128)}, f32[768,128]{1,0:T(8,128)S(1)}, ...), condition=%wide.region_4.5_spmd.clone, body=%wide.region_1.4_spmd.clone.sunk | while | flops 415534848 | bytes 11033179 | solution.py:71
  439.2 1.6 fusion.37
  441.7 2.1 fusion.40
  444.1 1.6 fusion.37
  446.6 2.1 fusion.40
  448.9 1.6 fusion.37
  451.4 2.1 fusion.40
  453.8 1.6 fusion.37
  456.3 2.1 fusion.40
  458.6 1.6 fusion.37
  461.1 2.1 fusion.40
  463.5 1.6 fusion.37
  466.0 2.1 fusion.40
  468.3 1.6 fusion.37
  470.8 2.1 fusion.40
  473.2 1.6 fusion.37
  475.7 2.1 fusion.40
  478.0 1.6 fusion.37
  480.5 2.1 fusion.40
  482.9 1.6 fusion.37
  485.4 2.1 fusion.40
  487.7 1.6 fusion.37
  490.2 2.1 fusion.40
  492.6 1.6 fusion.37
  495.1 2.1 fusion.40
  497.4 1.6 fusion.37
  499.9 2.1 fusion.40
  504.8 2.1 fusion.40
  507.1 1.6 fusion.37
  509.6 2.1 fusion.40
  514.5 2.1 fusion.40
  516.8 1.6 fusion.37
  519.3 2.1 fusion.40
  521.7 1.6 fusion.37
  524.2 2.1 fusion.40
  526.5 1.6 fusion.37
  529.0 2.1 fusion.40
  533.9 2.1 fusion.40
  536.2 1.6 fusion.37
  538.7 2.1 fusion.40
  543.6 2.1 fusion.40
  545.9 1.6 fusion.37
  548.4 2.1 fusion.40
  550.8 1.6 fusion.37
  553.3 2.1 fusion.40
  (189 shorter events, 36.5 us)
Async XLA Ops:
  7.2 431.9 %all-gather.2.cloned.1.call-start = ((), (), s32[]{:S(2)}) async-start(), calls=%async_computation | async-start | bytes 12632064 | tf_op jit(solution)/shard_map/all_gather | solution.py:54
Sparse Core Ops, SparseCore 0:
  10.5 428.5 all-gather.1
where the time goes:
time: 566 us; the launch traced here: 564 us
  waiting for transfers between devices  332 us (59%)
  matrix products  88.6 us (16%)
  blocking collectives  81.4 us (14%)
  other arithmetic  38.2 us (7%)
  between operations  14.8 us (3%)
  local copies, waits for them, and re-layouts  6.88 us (1%)
    all_gather x1, waiting for transfers between devices, local(): key_piece = lax.all_gather(paired, ('row', 'col'), axis=0, tiled=True)  332 us
    unnamed x1, blocking collectives  81.4 us
    dot_general x24, matrix products, update(): jnp.dot(weights.astype(jnp.bfloat16), value_part, preferred_element_type=...  51.1 us
    dot_general x24, matrix products, update(): lax.dot_general(query_rows, key_part, (((1,), (1,)), ((), ())), preferred...  37.5 us
    reduce_sum x24, other arithmetic, update(): total = total * rescale + jnp.sum(weights, axis=1)  21.3 us
    reduce_sum x1, other arithmetic, local(): jnp.sum(jnp.where(owner[:, None] == block_ids[None, :], all_starts[None,...  14.9 us
  transfers between devices with their start and end apart: 1, of which 1 were waited for; matrix products, arithmetic and copies ran while one was open for 3% of the time, Pallas kernels for 0%

commit v1 on v0

v1 whole, which is shorter than its diff:
```python
import functools
import math

import jax
import jax.numpy as jnp
from jax import lax
from jax.experimental import pallas as pl
from jax.experimental.pallas import tpu as pltpu
from jax.sharding import PartitionSpec as P

MESH = pl.DeviceIdType.MESH
TOK = 96
HD = 128
HALF = 4 * TOK
MSG = 2 * TOK + 16
QMSG = HALF + 16
OMSG = HALF + TOK
ROWS = 2 * HALF
KEYS = 8 * TOK
REL = (0, 1, 3, 2)
INV = (0, 2, 1, 3)
GROUPS = ((0, 1), (1, 2), (3, 1))
SCALE = HD ** -0.5
C2 = SCALE * math.log2(math.e)
MASKED = -1e30
FLOOR = -1e20


def kernel(start_ref, q_ref, k_ref, v_ref, att_ref, lt_ref, kv, qb, qother, ob, rb, acc, peak,
           s_a, s_b, p_a, p_b, f_a, f_b,
           y_s, y_r, own_s, own_r, z_s, z_r, hand_s, hand_r, handy_s, handy_r, q_s, q_r, o_s, o_r):
    row = lax.axis_index("row")
    col = lax.axis_index("col")
    x = lax.rem(row, 4)
    y = lax.div(col, 16) * 2 + lax.div(row, 4)
    z = lax.rem(lax.div(col, 2), 8)
    c = lax.rem(col, 2)

    def device(xx, yy, zz, cc):
        return (lax.rem(yy, 2) * 4 + xx, (lax.div(yy, 2) * 8 + zz) * 2 + cc)

    partner = device(x, y, z, 1 - c)
    y_peer = [None] + [device(x, lax.rem(y + REL[k], 4), z, c) for k in (1, 2, 3)]
    z_up = device(x, y, lax.rem(z + 1, 8), c)
    z_down = device(x, y, lax.rem(z + 7, 8), c)
    x_peer = [[None, partner]] + [
        [device(lax.rem(x + REL[k], 4), y, z, c), device(lax.rem(x + REL[k], 4), y, z, 1 - c)]
        for k in (1, 2, 3)
    ]

    barrier = pltpu.get_barrier_semaphore()
    peers = [partner, z_up, z_down] + y_peer[1:] + x_peer[1] + x_peer[2] + x_peer[3]
    for peer in peers:
        pl.semaphore_signal(barrier, inc=1, device_id=peer, device_id_type=MESH)

    number = jnp.full((16, HD), start_ref[0].astype(jnp.float32), jnp.float32).astype(jnp.bfloat16)
    kv[0, 0, 0:TOK, :] = k_ref[...]
    kv[0, 0, TOK:2 * TOK, :] = v_ref[...]
    kv[0, 0, 2 * TOK:MSG, :] = number
    for h in range(4):
        here = pl.ds(pl.multiple_of((c * 4 + h) * HD, HD), HD)
        there = pl.ds(pl.multiple_of(((1 - c) * 4 + h) * HD, HD), HD)
        qb[0, 0, h * TOK:(h + 1) * TOK, :] = q_ref[:, here]
        qother[h * TOK:(h + 1) * TOK, :] = q_ref[:, there]
    qb[0, 0, HALF:QMSG, :] = number
    qother[HALF:QMSG, :] = number
    acc[...] = jnp.zeros_like(acc)
    peak[...] = jnp.full(peak.shape, FLOOR, jnp.float32)

    def copy(src, dst, send, recv, to):
        return pltpu.make_async_remote_copy(
            src_ref=src, dst_ref=dst, send_sem=send, recv_sem=recv, device_id=to, device_id_type=MESH
        )

    sent = []

    def start(make, *which):
        make(*which).start()
        sent.append((make, which))

    def q_copy(k, other):
        if other:
            return copy(qother, qb.at[INV[k], 1], q_s.at[k, 1], q_r.at[INV[k], 1], x_peer[k][1])
        return copy(qb.at[0, 0], qb.at[INV[k], 0], q_s.at[k, 0], q_r.at[INV[k], 0], x_peer[k][0])

    def q_wait(k, other):
        copy(qb.at[k, other], qb.at[k, other], q_s.at[k, other], q_r.at[k, other], partner).wait_recv()

    def y_copy(k):
        return copy(kv.at[0, 0], kv.at[0, INV[k]], y_s.at[k], y_r.at[INV[k]], y_peer[k])

    def y_wait(k):
        copy(kv.at[0, k], kv.at[0, k], y_s.at[k], y_r.at[k], partner).wait_recv()

    def part(slot, g):
        return kv.at[slot, pl.ds(GROUPS[g][0], GROUPS[g][1])]

    def z_copy(slot, g):
        src = 0 if slot <= 2 else slot - 2
        to = z_up if slot % 2 == 1 else z_down
        return copy(part(src, g), part(slot, g), z_s.at[slot, g], z_r.at[slot, g], to)

    def opposite_copy(g):
        to = device(x, y, lax.rem(z + 1 + 6 * c, 8), c)
        return copy(part(5 + c, g), part(7, g), z_s.at[7, g], z_r.at[7, g], to)

    def z_wait(slot, g):
        copy(part(slot, g), part(slot, g), z_s.at[slot, g], z_r.at[slot, g], partner).wait_recv()

    def hand_copy(slot, g):
        dst = kv.at[slot, pl.ds(4 + GROUPS[g][0], GROUPS[g][1])]
        return copy(part(slot, g), dst, hand_s.at[slot, g], hand_r.at[slot, g], partner)

    def hand_wait(slot):
        for g in range(3):
            dst = kv.at[slot, pl.ds(4 + GROUPS[g][0], GROUPS[g][1])]
            copy(dst, dst, hand_s.at[slot, g], hand_r.at[slot, g], partner).wait_recv()

    def arrive(slots, g):
        for slot in slots:
            z_wait(slot, g)
            if slot + 2 <= 6:
                start(z_copy, slot + 2, g)
            start(hand_copy, slot, g)
        if 5 in slots:
            start(opposite_copy, g)

    def own_copy():
        return copy(kv.at[0, 0], kv.at[0, 4], own_s, own_r, partner)

    def row_copy():
        return copy(kv.at[0, pl.ds(1, 3)], kv.at[0, pl.ds(5, 3)], handy_s, handy_r, partner)

    def o_copy(k, other):
        return copy(ob.at[k, other], rb.at[INV[k], other], o_s.at[k, other], o_r.at[INV[k], other], x_peer[k][other])

    def o_wait(k, other):
        copy(rb.at[k, other], rb.at[k, other], o_s.at[k, other], o_r.at[k, other], partner).wait_recv()

    def unit(u):
        if isinstance(u, int):
            a, b = divmod(u + 2, 3)
            if u < 4:
                return u, 0
            if u < 16:
                return b + 1, a - 1
            if u < 25:
                return 9 - a, 5 + b
            return 0, u - 24
        a, b = lax.div(u + 2, 3), lax.rem(u + 2, 3)
        from4, from16, from25 = lax.div(u + 28, 32), lax.div(u + 16, 32), lax.div(u + 7, 32)
        query = (1 - from4) * u + (from4 - from16) * (b + 1) + (from16 - from25) * (9 - a)
        slot = (from4 - from16) * (a - 1) + (from16 - from25) * (5 + b) + from25 * (u - 24)
        return query, slot

    lane = lax.broadcasted_iota(jnp.int32, (1, HD), 1)
    ones = jnp.ones((KEYS, HD), jnp.bfloat16)

    def scores(u, s):
        query, slot = unit(u)
        rows = qb[query, :, 0:HALF, :].reshape(ROWS, HD)
        keys = kv[slot, :, 0:TOK, :].reshape(KEYS, HD)
        s[...] = lax.dot_general(rows, keys, (((1,), (1,)), ((), ())), preferred_element_type=jnp.float32)

    def soften(u, s, p, f, diagonal=False):
        query, slot = unit(u)
        numbers = [kv[slot, i, 2 * TOK:MSG, :].astype(jnp.float32)[0:1, :] for i in range(8)]
        tiles = []
        for t in range(KEYS // HD):
            first = t * HD // TOK
            edge = (first + 1) * TOK - t * HD
            tiles.append(jnp.where(lane < edge, numbers[first], numbers[first + 1]))
        blocks = jnp.concatenate(tiles, axis=1)
        for half in range(2):
            at = pl.ds(half * HALF, HALF)
            mine = qb[query, half, HALF:QMSG, :].astype(jnp.float32)[0:1, :]
            mine = jnp.concatenate([mine] * (KEYS // HD), axis=1)
            v = s[at, :] + jnp.where(blocks > mine, MASKED, 0.0)
            if diagonal:
                key = lax.broadcasted_iota(jnp.int32, (HALF, KEYS), 1)
                token = lax.rem(lax.broadcasted_iota(jnp.int32, (HALF, KEYS), 0), TOK)
                begin = half * 4 * TOK
                later = (key >= begin) & (key < begin + TOK) & (key - begin > token)
                v = jnp.where(later, MASKED, v)
            old = peak[query, at, :]
            new = jnp.maximum(old, jnp.max(v, axis=1, keepdims=True))
            p[at, :] = jnp.exp2((v - new[:, :1]) * C2).astype(jnp.bfloat16)
            f[at, :] = jnp.exp2((old - new) * C2)
            peak[query, at, :] = new

    def gather(u, p, f):
        query, slot = unit(u)
        vals = kv[slot, :, TOK:2 * TOK, :].reshape(KEYS, HD)
        vals = jnp.concatenate([vals, ones], axis=1)
        factor = jnp.concatenate([f[...], f[...]], axis=1)
        acc[query] = acc[query] * factor + jnp.dot(p[...], vals, preferred_element_type=jnp.float32)

    def finish(k):
        for half in range(2):
            at = pl.ds(half * HALF, HALF)
            total = acc[k, at, HD:2 * HD]
            some = total > 0.0
            safe = jnp.where(some, total, 1.0)
            ob[k, half, 0:HALF, :] = (acc[k, at, 0:HD] / safe).astype(jnp.bfloat16)
            log = jnp.where(some, peak[k, at, :] * SCALE + jnp.log(safe), MASKED)
            hi = log.astype(jnp.bfloat16).astype(jnp.float32)
            mid = (log - hi).astype(jnp.bfloat16).astype(jnp.float32)
            low = log - hi - mid
            packed = jnp.zeros((TOK, HD), jnp.float32)
            for h in range(4):
                for i, term in enumerate((hi, mid, low)):
                    packed = jnp.where(lane == 3 * h + i, term[h * TOK:(h + 1) * TOK, :], packed)
            ob[k, half, HALF:OMSG, :] = packed.astype(jnp.bfloat16)

    def send_out(k):
        finish(k)
        for other in range(2):
            if k or other:
                start(o_copy, k, other)

    pl.semaphore_wait(barrier, len(peers))
    start(q_copy, 0, 1)
    start(own_copy)
    for k in (1, 2, 3):
        start(y_copy, k)
        if k < 3:
            start(z_copy, k, 0)
        for other in range(2):
            start(q_copy, k, other)
    for k in (1, 2):
        y_wait(k)
    start(z_copy, 1, 1)
    start(z_copy, 2, 1)
    y_wait(3)
    start(z_copy, 1, 2)
    start(z_copy, 2, 2)
    start(row_copy)
    own_copy().wait_recv()
    q_wait(0, 1)
    arrive((1, 2), 0)
    row_copy().wait_recv()
    scores(0, s_a)
    q_wait(1, 0)
    q_wait(1, 1)
    scores(1, s_b)
    soften(0, s_a, p_a, f_a, diagonal=True)

    def events(t):
        def at(step):
            return pl.when(t == step)

        @at(0)
        def _():
            for k in (2, 3):
                q_wait(k, 0)
                q_wait(k, 1)

        @at(1)
        def _():
            arrive((1, 2), 1)
            arrive((3, 4), 0)
            arrive((1, 2), 2)
            hand_wait(1)
            hand_wait(2)

        @at(3)
        def _():
            arrive((3, 4), 1)
            arrive((5, 6), 0)

        @at(4)
        def _():
            arrive((3, 4), 2)
            hand_wait(3)
            hand_wait(4)

        @at(6)
        def _():
            arrive((5, 6), 1)
            arrive((5, 6), 2)

        @at(7)
        def _():
            hand_wait(5)
            hand_wait(6)

        @at(8)
        def _():
            for g in range(3):
                z_wait(7, g)
                start(hand_copy, 7, g)
            hand_wait(7)

        @at(11)
        def _():
            send_out(3)

        @at(12)
        def _():
            send_out(2)

        @at(14)
        def _():
            send_out(1)

    def turn(t, carry):
        events(t)
        i = 2 * t + 1
        scores(i + 1, s_a)
        soften(i, s_b, p_b, f_b)
        gather(i - 1, p_a, f_a)
        scores(i + 2, s_b)
        soften(i + 1, s_a, p_a, f_a)
        gather(i, p_b, f_b)
        return carry

    lax.fori_loop(0, 15, turn, 0)
    soften(31, s_b, p_b, f_b)
    gather(30, p_a, f_a)
    gather(31, p_b, f_b)
    send_out(0)

    for make, which in sent:
        make(*which).wait_send()
    for k in range(4):
        for other in range(2):
            if k or other:
                o_wait(k, other)

    totals = jnp.zeros((TOK, HD), jnp.float32)
    for other in range(2):
        half = c if other == 0 else 1 - c
        parts = [ob.at[0, 0] if k == 0 and other == 0 else rb.at[k, other] for k in range(4)]
        logs = [part_ref[HALF:OMSG, :].astype(jnp.float32) for part_ref in parts]
        for h in range(4):
            log = [v[:, 3 * h:3 * h + 1] + v[:, 3 * h + 1:3 * h + 2] + v[:, 3 * h + 2:3 * h + 3] for v in logs]
            most = jnp.maximum(jnp.maximum(log[0], log[1]), jnp.maximum(log[2], log[3]))
            share = [jnp.exp(v - most) for v in log]
            whole = share[0] + share[1] + share[2] + share[3]
            mixed = jnp.zeros((TOK, HD), jnp.float32)
            for k in range(4):
                mixed += (share[k] / whole) * parts[k][h * TOK:(h + 1) * TOK, :].astype(jnp.float32)
            att_ref[:, pl.ds(pl.multiple_of((half * 4 + h) * HD, HD), HD)] = mixed
            totals = jnp.where(lane == half * 4 + h, most + jnp.log(whole), totals)
    lt_ref[...] = totals[:, 0:8]


def local(queries, keys, values, block_start):
    vmem = pl.BlockSpec(memory_space=pltpu.VMEM)
    dma = pltpu.SemaphoreType.DMA
    bf16, f32 = jnp.bfloat16, jnp.float32
    return pl.pallas_call(
        kernel,
        out_shape=(
            jax.ShapeDtypeStruct((TOK, 8 * HD), f32),
            jax.ShapeDtypeStruct((TOK, 8), f32),
        ),
        in_specs=[pl.BlockSpec(memory_space=pltpu.SMEM), vmem, vmem, vmem],
        out_specs=(vmem, vmem),
        scratch_shapes=[
            pltpu.VMEM((8, 8, MSG, HD), bf16),
            pltpu.VMEM((4, 2, QMSG, HD), bf16),
            pltpu.VMEM((QMSG, HD), bf16),
            pltpu.VMEM((4, 2, OMSG, HD), bf16),
            pltpu.VMEM((4, 2, OMSG, HD), bf16),
            pltpu.VMEM((4, ROWS, 2 * HD), f32),
            pltpu.VMEM((4, ROWS, HD), f32),
            pltpu.VMEM((ROWS, KEYS), f32),
            pltpu.VMEM((ROWS, KEYS), f32),
            pltpu.VMEM((ROWS, KEYS), bf16),
            pltpu.VMEM((ROWS, KEYS), bf16),
            pltpu.VMEM((ROWS, HD), f32),
            pltpu.VMEM((ROWS, HD), f32),
            dma((4,)), dma((4,)), dma, dma, dma((8, 3)), dma((8, 3)), dma((8, 3)), dma((8, 3)), dma, dma,
            dma((4, 2)), dma((4, 2)), dma((4, 2)), dma((4, 2)),
        ],
        compiler_params=pltpu.CompilerParams(
            collective_id=0, has_side_effects=True, vmem_limit_bytes=48 << 20
        ),
    )(block_start, queries, keys, values)


def solution(mesh):
    placed = (
        P(("row", "col"), None),
        P(("row", "col"), None),
        P(("row", "col"), None),
        P(("row", "col")),
    )
    return jax.shard_map(
        local,
        mesh=mesh,
        in_specs=placed,
        out_specs=(P(("row", "col"), None), P(("row", "col"), None)),
        check_vma=False,
    )
```

time: 566 us -> 67.9 us (0.12)
  waiting for transfers between devices: 332 us -> 0 us
  matrix products: 88.6 us -> 0 us
  blocking collectives: 81.4 us -> 0 us
  Pallas kernels: 0 us -> 62.5 us
  other arithmetic: 38.2 us -> 0 us
  between operations: 14.8 us -> 1.3 us
    all_gather x1 -> x0, waiting for transfers between devices: 332 us -> none  [local(): key_piece = lax.all_gather(paired, ('row', 'col'), axis=0, tiled=True)]
    dot_general x48 -> x0, matrix products: 88.6 us -> none  [the longest x24 51.1 us: update(): jnp.dot(weights.astype(jnp.bfloat16), value_part, preferred_element_type=...]
    unnamed x1 -> x0, blocking collectives: 81.4 us -> none
    pallas_call x0 -> x1, Pallas kernels: none -> 62.5 us  [local(): pl.pallas_call(kernel, out_shape=(jax.ShapeDtypeStruct((TOK, 8 * HD), f32...]
    reduce_sum x25 -> x0, other arithmetic: 36.2 us -> none  [the longest x24 21.3 us: update(): total = total * rescale + jnp.sum(weights, axis=1)]
  transfers between devices with their start and end apart: 1 -> 0, of which waited for: 1 -> 0; matrix products, arithmetic and copies ran while one was open for 3% -> 0% of each run, Pallas kernels for 0% -> 0%
where the time goes in v1:
time: 67.9 us; the launch traced here: 67.6 us
  Pallas kernels  62.5 us (92%)
  local copies, waits for them, and re-layouts  3.8 us (6%)
  between operations  1.3 us (2%)
    pallas_call x1, Pallas kernels, local(): pl.pallas_call(kernel, out_shape=(jax.ShapeDtypeStruct((TOK, 8 * HD), f32...  62.5 us
    unnamed x7, local copies, waits for them, and re-layouts  3.14 us

profile of v1, /device:TPU:1, one launch (start us, length us, event | category | flops | bytes accessed | tf_op | source)
XLA Modules:
  0.0 67.6 jit_solution(2186127877346833291)
XLA Ops:
  1.3 0.0 copy-start
  1.3 0.9 %copy-done = bf16[96,1024]{1,0:T(8,128)(2,1)S(1)} copy-done((bf16[96,1024]{1,0:T(8,128)(2,1)S(1)}, bf16[96,1024]{1,0:T(8,128)(2,1)}, u32[]{:S(2)}) %copy-start) | copy-done | bytes 196632
  2.2 0.0 copy-start.1
  2.2 0.7 %copy-done.1 = bf16[96,128]{1,0:T(8,128)(2,1)S(1)} copy-done((bf16[96,128]{1,0:T(8,128)(2,1)S(1)}, bf16[96,128]{1,0:T(8,128)(2,1)}, u32[]{:S(2)}) %copy-start.1) | copy-done | bytes 24600
  2.9 0.0 copy-start.2
  2.9 0.7 %copy-done.2 = bf16[96,128]{1,0:T(8,128)(2,1)S(1)} copy-done((bf16[96,128]{1,0:T(8,128)(2,1)S(1)}, bf16[96,128]{1,0:T(8,128)(2,1)}, u32[]{:S(2)}) %copy-start.2) | copy-done | bytes 24600
  3.7 62.5 %shard_map.59 = (f32[96,1024]{1,0:T(8,128)S(1)}, f32[96,8]{1,0:T(8,128)S(1)}) custom-call(s32[1]{0:T(128)S(6)} %copy.8.start_ref, bf16[96,1024]{1,0:T(8,128)(2,1)S(1)} %copy-done, bf16[96,128]{1,0:T(8,128)(2,1)S(1)} %copy-done.1, bf16[96,128]{1,0:T(8,128)(2,1)S(1)} %copy-done.2), custom_call_target="tpu_custom_call" | custom-call | tf_op jit(solution)/shard_map/pallas_call | solution.py:352
  66.2 0.7 copy.6
  66.9 0.7 %copy.9 = f32[96,1024]{1,0:T(8,128)} copy(f32[96,1024]{1,0:T(8,128)S(1)} %get-tuple-element.6) | data formatting | bytes 786432
Async XLA Ops:
  1.3 0.9 %copy-start = (bf16[96,1024]{1,0:T(8,128)(2,1)S(1)}, bf16[96,1024]{1,0:T(8,128)(2,1)}, u32[]{:S(2)}) copy-start(bf16[96,1024]{1,0:T(8,128)(2,1)} %q_ref.1) | copy-start | bytes 589828
  2.2 0.7 %copy-start.1 = (bf16[96,128]{1,0:T(8,128)(2,1)S(1)}, bf16[96,128]{1,0:T(8,128)(2,1)}, u32[]{:S(2)}) copy-start(bf16[96,128]{1,0:T(8,128)(2,1)} %k_ref.1) | copy-start | bytes 73732
  2.9 0.7 %copy-start.2 = (bf16[96,128]{1,0:T(8,128)(2,1)S(1)}, bf16[96,128]{1,0:T(8,128)(2,1)}, u32[]{:S(2)}) copy-start(bf16[96,128]{1,0:T(8,128)(2,1)} %v_ref.1) | copy-start | bytes 73732

commit v2 on v1

v2 whole, which is shorter than its diff:
```python
import functools
import math

import jax
import jax.numpy as jnp
from jax import lax
from jax.experimental import pallas as pl
from jax.experimental.pallas import tpu as pltpu
from jax.sharding import PartitionSpec as P

MESH = pl.DeviceIdType.MESH
TOK = 96
HD = 128
HALF = 4 * TOK
MSG = 2 * TOK + 16
QMSG = HALF + 16
OMSG = HALF + TOK
ROWS = 2 * HALF
KEYS = 8 * TOK
REL = (0, 1, 3, 2)
INV = (0, 2, 1, 3)
Z_OFF = (0, 1, 7, 2, 6, 3, 5, 4)
Z_INV = (0, 2, 1, 4, 3, 6, 5, 7)
PLANE_AT = (1, 1, 2, 2, 5, 5, 7, 7)
LINE_AT = (0, 3, 4, 6)
SCALE = HD ** -0.5
C2 = SCALE * math.log2(math.e)
MASKED = -1e30
FLOOR = -1e20


def kernel(start_ref, q_hbm, k_hbm, v_hbm, att_ref, lt_ref, q_ref, kv, qb, qother, ob, rb, acc, peak,
           marks, triangle, s_a, s_b, p_a, p_b, f_a, f_b,
           y_s, y_r, z_s, z_r, a_s, a_r, b_s, b_r, ah_s, bh_s, q_s, q_r, o_s, o_r, in_s):
    row = lax.axis_index("row")
    col = lax.axis_index("col")
    x = lax.rem(row, 4)
    y = lax.div(col, 16) * 2 + lax.div(row, 4)
    z = lax.rem(lax.div(col, 2), 8)
    c = lax.rem(col, 2)

    def device(xx, yy, zz, cc):
        return (lax.rem(yy, 2) * 4 + xx, (lax.div(yy, 2) * 8 + zz) * 2 + cc)

    partner = device(x, y, z, 1 - c)
    y_peer = [None] + [device(x, lax.rem(y + REL[k], 4), z, c) for k in (1, 2, 3)]
    z_up = device(x, y, lax.rem(z + 1, 8), c)
    z_down = device(x, y, lax.rem(z + 7, 8), c)
    z_peer = [device(x, y, lax.rem(z + step, 8), c) for step in Z_OFF]
    x_peer = [[None, partner]] + [
        [device(lax.rem(x + REL[k], 4), y, z, c), device(lax.rem(x + REL[k], 4), y, z, 1 - c)]
        for k in (1, 2, 3)
    ]

    barrier = pltpu.get_barrier_semaphore()

    def greet(peers):
        for peer in peers:
            pl.semaphore_signal(barrier, inc=1, device_id=peer, device_id_type=MESH)

    greet([partner, z_up, z_down, y_peer[1], y_peer[2]] + x_peer[1] + x_peer[2] + x_peer[3])

    @pl.when(c == 0)
    def _():
        greet([y_peer[3]])

    @pl.when(c == 1)
    def _():
        greet(z_peer[3:])

    loads = [
        pltpu.make_async_copy(k_hbm, kv.at[1 - c, 0, pl.ds(0, TOK)], in_s.at[0]),
        pltpu.make_async_copy(v_hbm, kv.at[1 - c, 0, pl.ds(TOK, TOK)], in_s.at[1]),
        pltpu.make_async_copy(q_hbm, q_ref, in_s.at[2]),
    ]
    for load in loads:
        load.start()
    acc[...] = jnp.zeros_like(acc)
    peak[...] = jnp.full(peak.shape, FLOOR, jnp.float32)

    number = jnp.full((16, HD), start_ref[0].astype(jnp.float32), jnp.float32).astype(jnp.bfloat16)
    kv[1 - c, 0, 2 * TOK:MSG, :] = number
    for load in loads:
        load.wait()
    for h in range(4):
        here = pl.ds(pl.multiple_of((c * 4 + h) * HD, HD), HD)
        there = pl.ds(pl.multiple_of(((1 - c) * 4 + h) * HD, HD), HD)
        qb[0, 0, h * TOK:(h + 1) * TOK, :] = q_ref[:, here]
        qother[h * TOK:(h + 1) * TOK, :] = q_ref[:, there]
    qb[0, 0, HALF:QMSG, :] = number
    qother[HALF:QMSG, :] = number

    def copy(src, dst, send, recv, to):
        return pltpu.make_async_remote_copy(
            src_ref=src, dst_ref=dst, send_sem=send, recv_sem=recv, device_id=to, device_id_type=MESH
        )

    sent = ([], [], [])

    def start(make, *which, on=2):
        make(*which).start()
        sent[on].append((make, which))

    def wait(dst, recv):
        copy(dst, dst, recv, recv, partner).wait_recv()

    def q_copy(k, other):
        if other:
            return copy(qother, qb.at[INV[k], 1], q_s.at[k, 1], q_r.at[INV[k], 1], x_peer[k][1])
        return copy(qb.at[0, 0], qb.at[INV[k], 0], q_s.at[k, 0], q_r.at[INV[k], 0], x_peer[k][0])

    def q_wait(k, other):
        copy(qb.at[k, other], qb.at[k, other], q_s.at[k, other], q_r.at[k, other], partner).wait_recv()

    def plane(k, g):
        return kv.at[PLANE_AT[k], pl.ds(k % 2 * 4 + 2 * g, 2)]

    def y_copy(k):
        return copy(kv.at[1, 0], kv.at[1, INV[k]], y_s.at[k], y_r.at[INV[k]], y_peer[k])

    def a_copy(k, g):
        if k == 7:
            return copy(plane(5 + g, g), plane(7, g), a_s.at[7, g], a_r.at[7, g], z_down if g else z_up)
        to = z_up if k % 2 == 1 else z_down
        return copy(plane(max(k - 2, 0), g), plane(k, g), a_s.at[k, g], a_r.at[k, g], to)

    def a_hand(k, g):
        return copy(plane(k, g), plane(k, g), ah_s.at[k, g], a_r.at[k, g], partner)

    def pass_a(k, g):
        wait(plane(k, g), a_r.at[k, g])
        if k <= 4:
            start(a_copy, k + 2, g, on=0)
        elif k == 5 + g:
            start(a_copy, 7, g, on=0)
        start(a_hand, k, g, on=0)

    def have_a(*planes):
        @pl.when(c == 1)
        def _():
            for k in planes:
                for g in range(2):
                    wait(plane(k, g), a_r.at[k, g])

    def line(k, g):
        return kv.at[LINE_AT[k], pl.ds(4 * g, 4)]

    def z_copy(k):
        return copy(kv.at[0, 0], kv.at[0, Z_INV[k]], z_s.at[k], z_r.at[Z_INV[k]], z_peer[k])

    def b_copy(k, g):
        if k == 3:
            return copy(line(1 + g, g), line(3, g), b_s.at[3, g], b_r.at[3, g], y_peer[1] if g else y_peer[2])
        return copy(line(0, g), line(INV[k], g), b_s.at[k, g], b_r.at[INV[k], g], y_peer[k])

    def b_hand(k, g):
        return copy(line(k, g), line(k, g), bh_s.at[k, g], b_r.at[k, g], partner)

    def pass_b(k, g):
        wait(line(k, g), b_r.at[k, g])
        if k == 1 + g:
            start(b_copy, 3, g, on=1)
        start(b_hand, k, g, on=1)

    def have_b(*lines):
        @pl.when(c == 0)
        def _():
            for k in lines:
                for g in range(2):
                    wait(line(k, g), b_r.at[k, g])

    def o_copy(k, other):
        return copy(ob.at[k, other], rb.at[INV[k], other], o_s.at[k, other], o_r.at[INV[k], other], x_peer[k][other])

    def o_wait(k, other):
        copy(rb.at[k, other], rb.at[k, other], o_s.at[k, other], o_r.at[k, other], partner).wait_recv()

    def unit(u):
        if isinstance(u, int):
            a, b = divmod(u + 2, 3)
            if u < 4:
                return u, 0
            if u < 16:
                return b + 1, a - 1
            if u < 25:
                return 9 - a, 5 + b
            return 0, u - 24
        a, b = lax.div(u + 2, 3), lax.rem(u + 2, 3)
        from4, from16, from25 = lax.div(u + 28, 32), lax.div(u + 16, 32), lax.div(u + 7, 32)
        query = (1 - from4) * u + (from4 - from16) * (b + 1) + (from16 - from25) * (9 - a)
        slot = (from4 - from16) * (a - 1) + (from16 - from25) * (5 + b) + from25 * (u - 24)
        return query, slot

    lane = lax.broadcasted_iota(jnp.int32, (1, HD), 1)
    ones = jnp.ones((KEYS, HD), jnp.bfloat16)

    key = lax.broadcasted_iota(jnp.int32, (KEYS, HD), 0)
    mark = lax.broadcasted_iota(jnp.int32, (KEYS, HD), 1)
    marked = (lax.div(key, TOK) == mark) & (mark < 8) | (key + 8 == mark) & (key < TOK)
    marks[...] = jnp.where(marked, 1.0, 0.0).astype(jnp.bfloat16)
    token = lax.rem(lax.broadcasted_iota(jnp.int32, (HALF, HD), 0), TOK)
    later = lax.broadcasted_iota(jnp.int32, (HALF, HD), 1) - 8 > token
    triangle[...] = jnp.where(later, MASKED, 0.0).astype(jnp.bfloat16)

    def number_of(ref):
        return ref[...].astype(jnp.float32)[0:1, :]

    def scores(u, s):
        query, slot = unit(u)
        numbers = [number_of(kv.at[slot, i, pl.ds(2 * TOK, 16)]) for i in range(8)]
        rows = []
        for half in range(2):
            mine = number_of(qb.at[query, half, pl.ds(HALF, 16)])
            hidden = jnp.zeros((1, HD), jnp.float32)
            for i in range(8):
                hidden = jnp.where((lane == i) & (numbers[i] > mine), MASKED, hidden)
            same = jnp.where(numbers[0] == mine, 1.0, 0.0).astype(jnp.bfloat16)
            hidden = triangle[...] * same + hidden.astype(jnp.bfloat16)
            rows.append(jnp.concatenate([qb[query, half, 0:HALF, :], hidden], axis=1))
        rows = jnp.concatenate(rows, axis=0)
        keys = jnp.concatenate([kv[slot, :, 0:TOK, :].reshape(KEYS, HD), marks[...]], axis=1)
        s[...] = lax.dot_general(rows, keys, (((1,), (1,)), ((), ())), preferred_element_type=jnp.float32)

    def soften(u, s, p, f):
        query, slot = unit(u)
        for half in range(2):
            at = pl.ds(half * HALF, HALF)
            v = s[at, :]
            old = peak[query, at, :]
            new = jnp.maximum(old, jnp.max(v, axis=1, keepdims=True))
            p[at, :] = jnp.exp2((v - new[:, :1]) * C2).astype(jnp.bfloat16)
            f[at, :] = jnp.exp2((old - new) * C2)
            peak[query, at, :] = new

    def gather(u, p, f):
        query, slot = unit(u)
        vals = kv[slot, :, TOK:2 * TOK, :].reshape(KEYS, HD)
        vals = jnp.concatenate([vals, ones], axis=1)
        factor = jnp.concatenate([f[...], f[...]], axis=1)
        acc[query] = acc[query] * factor + jnp.dot(p[...], vals, preferred_element_type=jnp.float32)

    def finish(k):
        for half in range(2):
            at = pl.ds(half * HALF, HALF)
            total = acc[k, at, HD:2 * HD]
            some = total > 0.0
            safe = jnp.where(some, total, 1.0)
            ob[k, half, 0:HALF, :] = (acc[k, at, 0:HD] / safe).astype(jnp.bfloat16)
            log = jnp.where(some, peak[k, at, :] * SCALE + jnp.log(safe), MASKED)
            hi = log.astype(jnp.bfloat16).astype(jnp.float32)
            mid = (log - hi).astype(jnp.bfloat16).astype(jnp.float32)
            low = log - hi - mid
            packed = jnp.zeros((TOK, HD), jnp.float32)
            for h in range(4):
                for i, term in enumerate((hi, mid, low)):
                    packed = jnp.where(lane == 3 * h + i, term[h * TOK:(h + 1) * TOK, :], packed)
            ob[k, half, HALF:OMSG, :] = packed.astype(jnp.bfloat16)

    def send_out(k):
        finish(k)
        for other in range(2):
            if k or other:
                start(o_copy, k, other)

    pl.semaphore_wait(barrier, 12 + 4 * c)
    start(q_copy, 0, 1)

    @pl.when(c == 0)
    def _():
        for k in (1, 2, 3):
            start(y_copy, k, on=0)

    @pl.when(c == 1)
    def _():
        for k in range(1, 8):
            start(z_copy, k, on=1)

    for k in (1, 2, 3):
        for other in range(2):
            start(q_copy, k, other)

    @pl.when(c == 0)
    def _():
        wait(kv.at[1, 1], y_r.at[1])
        start(a_copy, 1, 0, on=0)
        start(a_copy, 2, 0, on=0)
        start(a_hand, 0, 0, on=0)
        wait(kv.at[1, 2], y_r.at[2])
        wait(kv.at[1, 3], y_r.at[3])
        start(a_copy, 1, 1, on=0)
        start(a_copy, 2, 1, on=0)
        start(a_hand, 0, 1, on=0)

    @pl.when(c == 1)
    def _():
        for g in range(2):
            for k in range(max(4 * g, 1), 4 * g + 4):
                wait(kv.at[0, k], z_r.at[k])
            start(b_copy, 1, g, on=1)
            start(b_copy, 2, g, on=1)
            start(b_hand, 0, g, on=1)

    @pl.when(c == 0)
    def _():
        for g in range(2):
            for k in (1, 2):
                pass_a(k, g)

    have_b(0)
    q_wait(0, 1)
    scores(0, s_a)
    q_wait(1, 0)
    q_wait(1, 1)
    scores(1, s_b)
    soften(0, s_a, p_a, f_a)

    def events(t):
        def at(step, core=None):
            return pl.when(t == step) if core is None else pl.when((t == step) & (c == core))

        @at(0)
        def _():
            for k in (2, 3):
                q_wait(k, 0)
                q_wait(k, 1)

        @at(1)
        def _():
            have_a(0, 1)

        @at(2)
        def _():
            @pl.when(c == 0)
            def _():
                for g in range(2):
                    for k in (3, 4):
                        pass_a(k, g)

            have_a(2, 3)

        @at(3, 1)
        def _():
            for g in range(2):
                for k in (1, 2):
                    pass_b(k, g)

        @at(4)
        def _():
            @pl.when(c == 0)
            def _():
                for g in range(2):
                    for k in (5, 6):
                        pass_a(k, g)

            have_b(1)

        @at(5)
        def _():
            have_b(2)

        @at(6, 1)
        def _():
            for g in range(2):
                pass_b(3, g)

        @at(7)
        def _():
            @pl.when(c == 0)
            def _():
                for g in range(2):
                    pass_a(7, g)

            have_a(4, 5)
            have_b(3)

        @at(8)
        def _():
            have_a(6, 7)

        @at(11)
        def _():
            send_out(3)

        @at(12)
        def _():
            send_out(2)

        @at(14)
        def _():
            send_out(1)

    def turn(t, carry):
        events(t)
        i = 2 * t + 1
        scores(i + 1, s_a)
        soften(i, s_b, p_b, f_b)
        gather(i - 1, p_a, f_a)
        scores(i + 2, s_b)
        soften(i + 1, s_a, p_a, f_a)
        gather(i, p_b, f_b)
        return carry

    lax.fori_loop(0, 15, turn, 0)
    soften(31, s_b, p_b, f_b)
    gather(30, p_a, f_a)
    gather(31, p_b, f_b)
    send_out(0)

    for make, which in sent[2]:
        make(*which).wait_send()
    for core in range(2):
        @pl.when(c == core)
        def _():
            for make, which in sent[core]:
                make(*which).wait_send()
    for k in range(4):
        for other in range(2):
            if k or other:
                o_wait(k, other)

    totals = jnp.zeros((TOK, HD), jnp.float32)
    for other in range(2):
        half = c if other == 0 else 1 - c
        parts = [ob.at[0, 0] if k == 0 and other == 0 else rb.at[k, other] for k in range(4)]
        logs = [part_ref[HALF:OMSG, :].astype(jnp.float32) for part_ref in parts]
        for h in range(4):
            log = [v[:, 3 * h:3 * h + 1] + v[:, 3 * h + 1:3 * h + 2] + v[:, 3 * h + 2:3 * h + 3] for v in logs]
            most = jnp.maximum(jnp.maximum(log[0], log[1]), jnp.maximum(log[2], log[3]))
            share = [jnp.exp(v - most) for v in log]
            whole = share[0] + share[1] + share[2] + share[3]
            mixed = jnp.zeros((TOK, HD), jnp.float32)
            for k in range(4):
                mixed += (share[k] / whole) * parts[k][h * TOK:(h + 1) * TOK, :].astype(jnp.float32)
            att_ref[:, pl.ds(pl.multiple_of((half * 4 + h) * HD, HD), HD)] = mixed
            totals = jnp.where(lane == half * 4 + h, most + jnp.log(whole), totals)
    lt_ref[...] = totals[:, 0:8]


def local(queries, keys, values, block_start):
    vmem = pl.BlockSpec(memory_space=pltpu.VMEM)
    hbm = pl.BlockSpec(memory_space=pl.ANY)
    dma = pltpu.SemaphoreType.DMA
    bf16, f32 = jnp.bfloat16, jnp.float32
    return pl.pallas_call(
        kernel,
        out_shape=(
            jax.ShapeDtypeStruct((TOK, 8 * HD), f32),
            jax.ShapeDtypeStruct((TOK, 8), f32),
        ),
        in_specs=[pl.BlockSpec(memory_space=pltpu.SMEM), hbm, hbm, hbm],
        out_specs=(vmem, vmem),
        scratch_shapes=[
            pltpu.VMEM((TOK, 8 * HD), bf16),
            pltpu.VMEM((8, 8, MSG, HD), bf16),
            pltpu.VMEM((4, 2, QMSG, HD), bf16),
            pltpu.VMEM((QMSG, HD), bf16),
            pltpu.VMEM((4, 2, OMSG, HD), bf16),
            pltpu.VMEM((4, 2, OMSG, HD), bf16),
            pltpu.VMEM((4, ROWS, 2 * HD), f32),
            pltpu.VMEM((4, ROWS, HD), f32),
            pltpu.VMEM((KEYS, HD), bf16),
            pltpu.VMEM((HALF, HD), bf16),
            pltpu.VMEM((ROWS, KEYS), f32),
            pltpu.VMEM((ROWS, KEYS), f32),
            pltpu.VMEM((ROWS, KEYS), bf16),
            pltpu.VMEM((ROWS, KEYS), bf16),
            pltpu.VMEM((ROWS, HD), f32),
            pltpu.VMEM((ROWS, HD), f32),
            dma((4,)), dma((4,)), dma((8,)), dma((8,)), dma((8, 2)), dma((8, 2)),
            dma((4, 2)), dma((4, 2)), dma((8, 2)), dma((4, 2)),
            dma((4, 2)), dma((4, 2)), dma((4, 2)), dma((4, 2)), dma((3,)),
        ],
        compiler_params=pltpu.CompilerParams(
            collective_id=0, has_side_effects=True, vmem_limit_bytes=48 << 20
        ),
    )(block_start, queries, keys, values)


def solution(mesh):
    placed = (
        P(("row", "col"), None),
        P(("row", "col"), None),
        P(("row", "col"), None),
        P(("row", "col")),
    )
    return jax.shard_map(
        local,
        mesh=mesh,
        in_specs=placed,
        out_specs=(P(("row", "col"), None), P(("row", "col"), None)),
        check_vma=False,
    )
```

time: 67.9 us -> 63.7 us (0.938)
  Pallas kernels: 62.5 us -> 58.4 us
    pallas_call x1, Pallas kernels: 62.5 us -> 58.4 us  [local(): pl.pallas_call(kernel, out_shape=(jax.ShapeDtypeStruct((TOK, 8 * HD), f32...]
where the time goes in v2:
time: 63.7 us; the launch traced here: 63.5 us
  Pallas kernels  58.4 us (92%)
  local copies, waits for them, and re-layouts  3.8 us (6%)
  between operations  1.3 us (2%)
    pallas_call x1, Pallas kernels, local(): pl.pallas_call(kernel, out_shape=(jax.ShapeDtypeStruct((TOK, 8 * HD), f32...  58.4 us
    unnamed x7, local copies, waits for them, and re-layouts  3.14 us

profile of v2, /device:TPU:1, one launch (start us, length us, event | category | flops | bytes accessed | tf_op | source)
XLA Modules:
  0.0 63.5 jit_solution(15950480661031198837)
XLA Ops:
  1.3 0.0 copy-start
  1.3 0.9 %copy-done = bf16[96,1024]{1,0:T(8,128)(2,1)S(1)} copy-done((bf16[96,1024]{1,0:T(8,128)(2,1)S(1)}, bf16[96,1024]{1,0:T(8,128)(2,1)}, u32[]{:S(2)}) %copy-start) | copy-done | bytes 196632
  2.2 0.0 copy-start.1
  2.2 0.7 %copy-done.1 = bf16[96,128]{1,0:T(8,128)(2,1)S(1)} copy-done((bf16[96,128]{1,0:T(8,128)(2,1)S(1)}, bf16[96,128]{1,0:T(8,128)(2,1)}, u32[]{:S(2)}) %copy-start.1) | copy-done | bytes 24600
  2.9 0.0 copy-start.2
  2.9 0.7 %copy-done.2 = bf16[96,128]{1,0:T(8,128)(2,1)S(1)} copy-done((bf16[96,128]{1,0:T(8,128)(2,1)S(1)}, bf16[96,128]{1,0:T(8,128)(2,1)}, u32[]{:S(2)}) %copy-start.2) | copy-done | bytes 24600
  3.7 58.4 %shard_map.59 = (f32[96,1024]{1,0:T(8,128)S(1)}, f32[96,8]{1,0:T(8,128)S(1)}) custom-call(s32[1]{0:T(128)S(6)} %copy.8.start_ref, bf16[96,1024]{1,0:T(8,128)(2,1)S(1)} %copy-done, bf16[96,128]{1,0:T(8,128)(2,1)S(1)} %copy-done.1, bf16[96,128]{1,0:T(8,128)(2,1)S(1)} %copy-done.2), custom_call_target="tpu_custom_call" | custom-call | tf_op jit(solution)/shard_map/pallas_call | solution.py:444
  62.1 0.7 %copy.6 = f32[96,8]{0,1:T(8,128)} copy(f32[96,8]{1,0:T(8,128)S(1)} %get-tuple-element.3) | data formatting | bytes 6144 | tf_op jit(solution)/shard_map/pallas_call | solution.py:444
  62.7 0.7 %copy.9 = f32[96,1024]{1,0:T(8,128)} copy(f32[96,1024]{1,0:T(8,128)S(1)} %get-tuple-element.6) | data formatting | bytes 786432
Async XLA Ops:
  1.3 0.9 %copy-start = (bf16[96,1024]{1,0:T(8,128)(2,1)S(1)}, bf16[96,1024]{1,0:T(8,128)(2,1)}, u32[]{:S(2)}) copy-start(bf16[96,1024]{1,0:T(8,128)(2,1)} %q_hbm.1) | copy-start | bytes 589828
  2.2 0.7 %copy-start.1 = (bf16[96,128]{1,0:T(8,128)(2,1)S(1)}, bf16[96,128]{1,0:T(8,128)(2,1)}, u32[]{:S(2)}) copy-start(bf16[96,128]{1,0:T(8,128)(2,1)} %k_hbm.1) | copy-start | bytes 73732
  2.9 0.7 %copy-start.2 = (bf16[96,128]{1,0:T(8,128)(2,1)S(1)}, bf16[96,128]{1,0:T(8,128)(2,1)}, u32[]{:S(2)}) copy-start(bf16[96,128]{1,0:T(8,128)(2,1)} %v_hbm.1) | copy-start | bytes 73732

commit v3 on v2

--- a/solution.py
+++ b/solution.py
@@ -14,15 +14,16 @@
 HALF = 4 * TOK
 MSG = 2 * TOK + 16
 QMSG = HALF + 16
-OMSG = HALF + TOK
+OMSG = HALF + 16
 ROWS = 2 * HALF
 KEYS = 8 * TOK
 REL = (0, 1, 3, 2)
 INV = (0, 2, 1, 3)
 Z_OFF = (0, 1, 7, 2, 6, 3, 5, 4)
 Z_INV = (0, 2, 1, 4, 3, 6, 5, 7)
-PLANE_AT = (1, 1, 2, 2, 5, 5, 7, 7)
-LINE_AT = (0, 3, 4, 6)
+PLANE_AT = ((0, 0), (1, 4), (2, 0), (2, 4), (5, 0), (5, 4), (7, 0), (7, 4))
+Z_AT = ((1, 0), (0, 4), (0, 5), (0, 6), (0, 7), (1, 1), (1, 2), (1, 3))
+LINE_AT = (None, 3, 4, 6)
 SCALE = HD ** -0.5
 C2 = SCALE * math.log2(math.e)
 MASKED = -1e30
@@ -69,8 +70,8 @@
         greet(z_peer[3:])
 
     loads = [
-        pltpu.make_async_copy(k_hbm, kv.at[1 - c, 0, pl.ds(0, TOK)], in_s.at[0]),
-        pltpu.make_async_copy(v_hbm, kv.at[1 - c, 0, pl.ds(TOK, TOK)], in_s.at[1]),
+        pltpu.make_async_copy(k_hbm, kv.at[c, 0, pl.ds(0, TOK)], in_s.at[0]),
+        pltpu.make_async_copy(v_hbm, kv.at[c, 0, pl.ds(TOK, TOK)], in_s.at[1]),
         pltpu.make_async_copy(q_hbm, q_ref, in_s.at[2]),
     ]
     for load in loads:
@@ -79,7 +80,7 @@
     peak[...] = jnp.full(peak.shape, FLOOR, jnp.float32)
 
     number = jnp.full((16, HD), start_ref[0].astype(jnp.float32), jnp.float32).astype(jnp.bfloat16)
-    kv[1 - c, 0, 2 * TOK:MSG, :] = number
+    kv[c, 0, 2 * TOK:MSG, :] = number
     for load in loads:
         load.wait()
     for h in range(4):
@@ -113,10 +114,11 @@
         copy(qb.at[k, other], qb.at[k, other], q_s.at[k, other], q_r.at[k, other], partner).wait_recv()
 
     def plane(k, g):
-        return kv.at[PLANE_AT[k], pl.ds(k % 2 * 4 + 2 * g, 2)]
+        unit, first = PLANE_AT[k]
+        return kv.at[unit, pl.ds(first + 2 * g, 2)]
 
     def y_copy(k):
-        return copy(kv.at[1, 0], kv.at[1, INV[k]], y_s.at[k], y_r.at[INV[k]], y_peer[k])
+        return copy(kv.at[0, 0], kv.at[0, INV[k]], y_s.at[k], y_r.at[INV[k]], y_peer[k])
 
     def a_copy(k, g):
         if k == 7:
@@ -143,10 +145,12 @@
                     wait(plane(k, g), a_r.at[k, g])
 
     def line(k, g):
+        if k == 0:
+            return kv.at[g, pl.ds(4 - 4 * g, 4)]
         return kv.at[LINE_AT[k], pl.ds(4 * g, 4)]
 
     def z_copy(k):
-        return copy(kv.at[0, 0], kv.at[0, Z_INV[k]], z_s.at[k], z_r.at[Z_INV[k]], z_peer[k])
+        return copy(kv.at[1, 0], kv.at[Z_AT[Z_INV[k]]], z_s.at[k], z_r.at[Z_INV[k]], z_peer[k])
 
     def b_copy(k, g):
         if k == 3:
@@ -162,12 +166,11 @@
             start(b_copy, 3, g, on=1)
         start(b_hand, k, g, on=1)
 
-    def have_b(*lines):
+    def have_b(k, parts=(0, 1)):
         @pl.when(c == 0)
         def _():
-            for k in lines:
-                for g in range(2):
-                    wait(line(k, g), b_r.at[k, g])
+            for g in parts:
+                wait(line(k, g), b_r.at[k, g])
 
     def o_copy(k, other):
         return copy(ob.at[k, other], rb.at[INV[k], other], o_s.at[k, other], o_r.at[INV[k], other], x_peer[k][other])
@@ -177,18 +180,22 @@
 
     def unit(u):
         if isinstance(u, int):
-            a, b = divmod(u + 2, 3)
-            if u < 4:
-                return u, 0
-            if u < 16:
-                return b + 1, a - 1
-            if u < 25:
-                return 9 - a, 5 + b
+            if u < 8:
+                return u % 4, u // 4
+            if u < 14:
+                return (u + 1) % 3 + 1, (u + 1) // 3 - 1
+            if u < 26:
+                return 7 - (u + 2) // 4, 4 + (u + 2) % 4
             return 0, u - 24
-        a, b = lax.div(u + 2, 3), lax.rem(u + 2, 3)
-        from4, from16, from25 = lax.div(u + 28, 32), lax.div(u + 16, 32), lax.div(u + 7, 32)
-        query = (1 - from4) * u + (from4 - from16) * (b + 1) + (from16 - from25) * (9 - a)
-        slot = (from4 - from16) * (a - 1) + (from16 - from25) * (5 + b) + from25 * (u - 24)
+        from8, from14, from26 = (lax.div(u + 32 - n, 32) for n in (8, 14, 26))
+        query = (
+            (1 - from8) * lax.rem(u, 4)
+            + (from8 - from14) * (lax.rem(u + 1, 3) + 1) + (from14 - from26) * (7 - lax.div(u + 2, 4))
+        )
+        slot = (
+            (1 - from8) * lax.div(u, 4)
+            + (from8 - from14) * (lax.div(u + 1, 3) - 1) + (from14 - from26) * (4 + lax.rem(u + 2, 4)) + from26 * (u - 24)
+        )
         return query, slot
 
     lane = lax.broadcasted_iota(jnp.int32, (1, HD), 1)
@@ -254,7 +261,8 @@
             for h in range(4):
                 for i, term in enumerate((hi, mid, low)):
                     packed = jnp.where(lane == 3 * h + i, term[h * TOK:(h + 1) * TOK, :], packed)
-            ob[k, half, HALF:OMSG, :] = packed.astype(jnp.bfloat16)
+            packed = jnp.concatenate([packed, jnp.zeros((HD - TOK, HD), jnp.float32)], axis=0)
+            ob[k, half, HALF:OMSG, :] = packed.T[0:16, :].astype(jnp.bfloat16)
 
     def send_out(k):
         finish(k)
@@ -275,30 +283,48 @@
         for k in range(1, 8):
             start(z_copy, k, on=1)
 
-    for k in (1, 2, 3):
+    for k in (1, 2):
         for other in range(2):
             start(q_copy, k, other)
 
     @pl.when(c == 0)
     def _():
-        wait(kv.at[1, 1], y_r.at[1])
+        wait(kv.at[0, 1], y_r.at[1])
         start(a_copy, 1, 0, on=0)
         start(a_copy, 2, 0, on=0)
         start(a_hand, 0, 0, on=0)
-        wait(kv.at[1, 2], y_r.at[2])
-        wait(kv.at[1, 3], y_r.at[3])
+        wait(kv.at[0, 2], y_r.at[2])
+        wait(kv.at[0, 3], y_r.at[3])
         start(a_copy, 1, 1, on=0)
         start(a_copy, 2, 1, on=0)
         start(a_hand, 0, 1, on=0)
 
+    def line_done(g):
+        for k in (range(5, 8) if g else range(1, 5)):
+            wait(kv.at[Z_AT[k]], z_r.at[k])
+        start(b_copy, 1, g, on=1)
+        start(b_copy, 2, g, on=1)
+        start(b_hand, 0, g, on=1)
+
     @pl.when(c == 1)
     def _():
-        for g in range(2):
-            for k in range(max(4 * g, 1), 4 * g + 4):
-                wait(kv.at[0, k], z_r.at[k])
-            start(b_copy, 1, g, on=1)
-            start(b_copy, 2, g, on=1)
-            start(b_hand, 0, g, on=1)
+        line_done(0)
+
+    for other in range(2):
+        start(q_copy, 3, other)
+    have_a(0)
+    have_b(0, (0,))
+    q_wait(0, 1)
+    scores(0, s_a)
+    soften(0, s_a, p_a, f_a)
+    q_wait(1, 0)
+    q_wait(1, 1)
+    scores(1, s_b)
+    q_wait(2, 0)
+    q_wait(2, 1)
+    scores(2, s_a)
+    soften(1, s_b, p_b, f_b)
+    gather(0, p_a, f_a)
 
     @pl.when(c == 0)
     def _():
@@ -306,86 +332,80 @@
             for k in (1, 2):
                 pass_a(k, g)
 
-    have_b(0)
-    q_wait(0, 1)
-    scores(0, s_a)
-    q_wait(1, 0)
-    q_wait(1, 1)
-    scores(1, s_b)
-    soften(0, s_a, p_a, f_a)
+    @pl.when(c == 1)
+    def _():
+        line_done(1)
+
+    q_wait(3, 0)
+    q_wait(3, 1)
+    scores(3, s_b)
+    soften(2, s_a, p_a, f_a)
+    gather(1, p_b, f_b)
 
     def events(t):
         def at(step, core=None):
             return pl.when(t == step) if core is None else pl.when((t == step) & (c == core))
 
-        @at(0)
-        def _():
-            for k in (2, 3):
-                q_wait(k, 0)
-                q_wait(k, 1)
-
         @at(1)
         def _():
-            have_a(0, 1)
-
-        @at(2)
-        def _():
-            @pl.when(c == 0)
-            def _():
-                for g in range(2):
-                    for k in (3, 4):
-                        pass_a(k, g)
-
-            have_a(2, 3)
-
-        @at(3, 1)
+            have_a(1)
+            have_b(0, (1,))
+
+        @at(1, 0)
+        def _():
+            for g in range(2):
+                for k in (3, 4):
+                    pass_a(k, g)
+
+        @at(2, 1)
         def _():
             for g in range(2):
                 for k in (1, 2):
                     pass_b(k, g)
 
+        @at(3, 0)
+        def _():
+            for g in range(2):
+                for k in (5, 6):
+                    pass_a(k, g)
+
+        @at(3)
+        def _():
+            have_a(2, 3)
+
         @at(4)
         def _():
-            @pl.when(c == 0)
-            def _():
-                for g in range(2):
-                    for k in (5, 6):
-                        pass_a(k, g)
-
             have_b(1)
 
-        @at(5)
-        def _():
-            have_b(2)
-
-        @at(6, 1)
+        @at(4, 1)
         def _():
             for g in range(2):
                 pass_b(3, g)
 
+        @at(5, 0)
+        def _():
+            for g in range(2):
+                pass_a(7, g)
+
+        @at(6)
+        def _():
+            have_b(2)
+            have_a(4, 5)
+
         @at(7)
         def _():
-            @pl.when(c == 0)
-            def _():
-                for g in range(2):
-                    pass_a(7, g)
-
-            have_a(4, 5)
             have_b(3)
-
-        @at(8)
-        def _():
             have_a(6, 7)
 
+        @at(9)
+        def _():
+            send_out(3)
+
         @at(11)
         def _():
-            send_out(3)
-
-        @at(12)
-        def _():
             send_out(2)
 
-        @at(14)
+        @at(13)
         def _():
             send_out(1)
 
@@ -400,7 +420,7 @@
         gather(i, p_b, f_b)
         return carry
 
-    lax.fori_loop(0, 15, turn, 0)
+    lax.fori_loop(1, 15, turn, 0)
     soften(31, s_b, p_b, f_b)
     gather(30, p_a, f_a)
     gather(31, p_b, f_b)
@@ -418,22 +438,29 @@
             if k or other:
                 o_wait(k, other)
 
-    totals = jnp.zeros((TOK, HD), jnp.float32)
+    sub = lax.broadcasted_iota(jnp.int32, (16, HD), 0)
+    totals = jnp.zeros((16, HD), jnp.float32)
     for other in range(2):
         half = c if other == 0 else 1 - c
         parts = [ob.at[0, 0] if k == 0 and other == 0 else rb.at[k, other] for k in range(4)]
         logs = [part_ref[HALF:OMSG, :].astype(jnp.float32) for part_ref in parts]
+        shares = jnp.zeros((16, HD), jnp.float32)
         for h in range(4):
-            log = [v[:, 3 * h:3 * h + 1] + v[:, 3 * h + 1:3 * h + 2] + v[:, 3 * h + 2:3 * h + 3] for v in logs]
+            log = [v[3 * h:3 * h + 1, :] + v[3 * h + 1:3 * h + 2, :] + v[3 * h + 2:3 * h + 3, :] for v in logs]
             most = jnp.maximum(jnp.maximum(log[0], log[1]), jnp.maximum(log[2], log[3]))
             share = [jnp.exp(v - most) for v in log]
             whole = share[0] + share[1] + share[2] + share[3]
+            for k in range(4):
+                shares = jnp.where(sub == 4 * h + k, share[k] / whole, shares)
+            totals = jnp.where(sub == half * 4 + h, most + jnp.log(whole), totals)
+        shares = jnp.concatenate([shares, jnp.zeros((HD - 16, HD), jnp.float32)], axis=0).T
+        for h in range(4):
             mixed = jnp.zeros((TOK, HD), jnp.float32)
             for k in range(4):
-                mixed += (share[k] / whole) * parts[k][h * TOK:(h + 1) * TOK, :].astype(jnp.float32)
+                share = shares[0:TOK, 4 * h + k:4 * h + k + 1]
+                mixed += share * parts[k][h * TOK:(h + 1) * TOK, :].astype(jnp.float32)
             att_ref[:, pl.ds(pl.multiple_of((half * 4 + h) * HD, HD), HD)] = mixed
-            totals = jnp.where(lane == half * 4 + h, most + jnp.log(whole), totals)
-    lt_ref[...] = totals[:, 0:8]
+    lt_ref[...] = totals[0:8, 0:TOK]
 
 
 def local(queries, keys, values, block_start):
@@ -441,11 +468,11 @@
     hbm = pl.BlockSpec(memory_space=pl.ANY)
     dma = pltpu.SemaphoreType.DMA
     bf16, f32 = jnp.bfloat16, jnp.float32
-    return pl.pallas_call(
+    attended, log_total = pl.pallas_call(
         kernel,
         out_shape=(
             jax.ShapeDtypeStruct((TOK, 8 * HD), f32),
-            jax.ShapeDtypeStruct((TOK, 8), f32),
+            jax.ShapeDtypeStruct((8, TOK), f32),
         ),
         in_specs=[pl.BlockSpec(memory_space=pltpu.SMEM), hbm, hbm, hbm],
         out_specs=(vmem, vmem),
@@ -474,6 +501,7 @@
             collective_id=0, has_side_effects=True, vmem_limit_bytes=48 << 20
         ),
     )(block_start, queries, keys, values)
+    return attended, log_total.T
 
 
 def solution(mesh):

time: 63.7 us -> 61 us (0.958)
  Pallas kernels: 58.4 us -> 55.4 us
    pallas_call x1, Pallas kernels: 58.4 us -> 55.4 us  [local(): pl.pallas_call(kernel, out_shape=(jax.ShapeDtypeStruct((TOK, 8 * HD), f32...]
    pallas_call x1 -> x0, local copies, waits for them, and re-layouts: 0.66 us -> none  [local(): pl.pallas_call(kernel, out_shape=(jax.ShapeDtypeStruct((TOK, 8 * HD), f32...]
    unnamed x7 -> x8, local copies, waits for them, and re-layouts: 3.14 us -> 3.73 us
where the time goes in v3:
time: 61 us; the launch traced here: 60.4 us
  Pallas kernels  55.4 us (91%)
  local copies, waits for them, and re-layouts  3.73 us (6%)
  between operations  1.3 us (2%)
    pallas_call x1, Pallas kernels, local(): pl.pallas_call(kernel, out_shape=(jax.ShapeDtypeStruct((TOK, 8 * HD), f32...  55.4 us
    unnamed x8, local copies, waits for them, and re-layouts  3.73 us

profile of v3, /device:TPU:1, one launch (start us, length us, event | category | flops | bytes accessed | tf_op | source)
XLA Modules:
  0.0 60.4 jit_solution(4658156783818606976)
XLA Ops:
  1.3 0.0 copy-start
  1.3 0.9 %copy-done = bf16[96,1024]{1,0:T(8,128)(2,1)S(1)} copy-done((bf16[96,1024]{1,0:T(8,128)(2,1)S(1)}, bf16[96,1024]{1,0:T(8,128)(2,1)}, u32[]{:S(2)}) %copy-start) | copy-done | bytes 196632
  2.2 0.0 copy-start.1
  2.2 0.7 %copy-done.1 = bf16[96,128]{1,0:T(8,128)(2,1)S(1)} copy-done((bf16[96,128]{1,0:T(8,128)(2,1)S(1)}, bf16[96,128]{1,0:T(8,128)(2,1)}, u32[]{:S(2)}) %copy-start.1) | copy-done | bytes 24600
  2.9 0.0 copy-start.2
  2.9 0.7 %copy-done.2 = bf16[96,128]{1,0:T(8,128)(2,1)S(1)} copy-done((bf16[96,128]{1,0:T(8,128)(2,1)S(1)}, bf16[96,128]{1,0:T(8,128)(2,1)}, u32[]{:S(2)}) %copy-start.2) | copy-done | bytes 24600
  3.7 55.4 %shard_map.59 = (f32[96,1024]{1,0:T(8,128)S(1)}, f32[8,96]{1,0:T(8,128)S(1)}) custom-call(s32[1]{0:T(128)S(6)} %copy.8.start_ref, bf16[96,1024]{1,0:T(8,128)(2,1)S(1)} %copy-done, bf16[96,128]{1,0:T(8,128)(2,1)S(1)} %copy-done.1, bf16[96,128]{1,0:T(8,128)(2,1)S(1)} %copy-done.2), custom_call_target="tpu_custom_call" | custom-call | tf_op jit(solution)/shard_map/pallas_call | solution.py:471
  59.1 0.7 %copy.9 = f32[96,1024]{1,0:T(8,128)} copy(f32[96,1024]{1,0:T(8,128)S(1)} %get-tuple-element.8) | data formatting | bytes 786432
  59.8 0.6 copy.10
Async XLA Ops:
  1.3 0.9 %copy-start = (bf16[96,1024]{1,0:T(8,128)(2,1)S(1)}, bf16[96,1024]{1,0:T(8,128)(2,1)}, u32[]{:S(2)}) copy-start(bf16[96,1024]{1,0:T(8,128)(2,1)} %q_hbm.1) | copy-start | bytes 589828
  2.2 0.7 %copy-start.1 = (bf16[96,128]{1,0:T(8,128)(2,1)S(1)}, bf16[96,128]{1,0:T(8,128)(2,1)}, u32[]{:S(2)}) copy-start(bf16[96,128]{1,0:T(8,128)(2,1)} %k_hbm.1) | copy-start | bytes 73732
  2.9 0.7 %copy-start.2 = (bf16[96,128]{1,0:T(8,128)(2,1)S(1)}, bf16[96,128]{1,0:T(8,128)(2,1)}, u32[]{:S(2)}) copy-start(bf16[96,128]{1,0:T(8,128)(2,1)} %v_hbm.1) | copy-start | bytes 73732

commit v4 on v3

--- a/solution.py
+++ b/solution.py
@@ -76,20 +76,11 @@
     ]
     for load in loads:
         load.start()
-    acc[...] = jnp.zeros_like(acc)
-    peak[...] = jnp.full(peak.shape, FLOOR, jnp.float32)
 
     number = jnp.full((16, HD), start_ref[0].astype(jnp.float32), jnp.float32).astype(jnp.bfloat16)
     kv[c, 0, 2 * TOK:MSG, :] = number
-    for load in loads:
+    for load in loads[:2]:
         load.wait()
-    for h in range(4):
-        here = pl.ds(pl.multiple_of((c * 4 + h) * HD, HD), HD)
-        there = pl.ds(pl.multiple_of(((1 - c) * 4 + h) * HD, HD), HD)
-        qb[0, 0, h * TOK:(h + 1) * TOK, :] = q_ref[:, here]
-        qother[h * TOK:(h + 1) * TOK, :] = q_ref[:, there]
-    qb[0, 0, HALF:QMSG, :] = number
-    qother[HALF:QMSG, :] = number
 
     def copy(src, dst, send, recv, to):
         return pltpu.make_async_remote_copy(
@@ -201,14 +192,6 @@
     lane = lax.broadcasted_iota(jnp.int32, (1, HD), 1)
     ones = jnp.ones((KEYS, HD), jnp.bfloat16)
 
-    key = lax.broadcasted_iota(jnp.int32, (KEYS, HD), 0)
-    mark = lax.broadcasted_iota(jnp.int32, (KEYS, HD), 1)
-    marked = (lax.div(key, TOK) == mark) & (mark < 8) | (key + 8 == mark) & (key < TOK)
-    marks[...] = jnp.where(marked, 1.0, 0.0).astype(jnp.bfloat16)
-    token = lax.rem(lax.broadcasted_iota(jnp.int32, (HALF, HD), 0), TOK)
-    later = lax.broadcasted_iota(jnp.int32, (HALF, HD), 1) - 8 > token
-    triangle[...] = jnp.where(later, MASKED, 0.0).astype(jnp.bfloat16)
-
     def number_of(ref):
         return ref[...].astype(jnp.float32)[0:1, :]
 
@@ -271,7 +254,6 @@
                 start(o_copy, k, other)
 
     pl.semaphore_wait(barrier, 12 + 4 * c)
-    start(q_copy, 0, 1)
 
     @pl.when(c == 0)
     def _():
@@ -283,9 +265,28 @@
         for k in range(1, 8):
             start(z_copy, k, on=1)
 
+    loads[2].wait()
+    for h in range(4):
+        here = pl.ds(pl.multiple_of((c * 4 + h) * HD, HD), HD)
+        there = pl.ds(pl.multiple_of(((1 - c) * 4 + h) * HD, HD), HD)
+        qb[0, 0, h * TOK:(h + 1) * TOK, :] = q_ref[:, here]
+        qother[h * TOK:(h + 1) * TOK, :] = q_ref[:, there]
+    qb[0, 0, HALF:QMSG, :] = number
+    qother[HALF:QMSG, :] = number
+    start(q_copy, 0, 1)
     for k in (1, 2):
         for other in range(2):
             start(q_copy, k, other)
+
+    acc[...] = jnp.zeros_like(acc)
+    peak[...] = jnp.full(peak.shape, FLOOR, jnp.float32)
+    key = lax.broadcasted_iota(jnp.int32, (KEYS, HD), 0)
+    mark = lax.broadcasted_iota(jnp.int32, (KEYS, HD), 1)
+    marked = (lax.div(key, TOK) == mark) & (mark < 8) | (key + 8 == mark) & (key < TOK)
+    marks[...] = jnp.where(marked, 1.0, 0.0).astype(jnp.bfloat16)
+    token = lax.rem(lax.broadcasted_iota(jnp.int32, (HALF, HD), 0), TOK)
+    later = lax.broadcasted_iota(jnp.int32, (HALF, HD), 1) - 8 > token
+    triangle[...] = jnp.where(later, MASKED, 0.0).astype(jnp.bfloat16)
 
     @pl.when(c == 0)
     def _():
@@ -351,19 +352,19 @@
             have_a(1)
             have_b(0, (1,))
 
-        @at(1, 0)
+        @at(2, 0)
         def _():
             for g in range(2):
                 for k in (3, 4):
                     pass_a(k, g)
 
-        @at(2, 1)
+        @at(3, 1)
         def _():
             for g in range(2):
                 for k in (1, 2):
                     pass_b(k, g)
 
-        @at(3, 0)
+        @at(4, 0)
         def _():
             for g in range(2):
                 for k in (5, 6):
@@ -377,12 +378,12 @@
         def _():
             have_b(1)
 
-        @at(4, 1)
+        @at(5, 1)
         def _():
             for g in range(2):
                 pass_b(3, g)
 
-        @at(5, 0)
+        @at(6, 0)
         def _():
             for g in range(2):
                 pass_a(7, g)

time: 61 us -> 60.7 us (level)
  no operation moved by 1% of the time
where the time goes in v4:
time: 60.7 us; the launch traced here: 60.4 us
  Pallas kernels  55.4 us (91%)
  local copies, waits for them, and re-layouts  3.73 us (6%)
  between operations  1.3 us (2%)
    pallas_call x1, Pallas kernels, local(): pl.pallas_call(kernel, out_shape=(jax.ShapeDtypeStruct((TOK, 8 * HD), f32...  55.4 us
    unnamed x8, local copies, waits for them, and re-layouts  3.73 us

profile of v4, /device:TPU:1, one launch (start us, length us, event | category | flops | bytes accessed | tf_op | source)
XLA Modules:
  0.0 60.4 jit_solution(8573729647565353160)
XLA Ops:
  1.3 0.0 copy-start
  1.3 0.9 %copy-done = bf16[96,1024]{1,0:T(8,128)(2,1)S(1)} copy-done((bf16[96,1024]{1,0:T(8,128)(2,1)S(1)}, bf16[96,1024]{1,0:T(8,128)(2,1)}, u32[]{:S(2)}) %copy-start) | copy-done | bytes 196632
  2.2 0.0 copy-start.1
  2.2 0.7 %copy-done.1 = bf16[96,128]{1,0:T(8,128)(2,1)S(1)} copy-done((bf16[96,128]{1,0:T(8,128)(2,1)S(1)}, bf16[96,128]{1,0:T(8,128)(2,1)}, u32[]{:S(2)}) %copy-start.1) | copy-done | bytes 24600
  2.9 0.0 copy-start.2
  2.9 0.7 %copy-done.2 = bf16[96,128]{1,0:T(8,128)(2,1)S(1)} copy-done((bf16[96,128]{1,0:T(8,128)(2,1)S(1)}, bf16[96,128]{1,0:T(8,128)(2,1)}, u32[]{:S(2)}) %copy-start.2) | copy-done | bytes 24600
  3.7 55.4 %shard_map.59 = (f32[96,1024]{1,0:T(8,128)S(1)}, f32[8,96]{1,0:T(8,128)S(1)}) custom-call(s32[1]{0:T(128)S(6)} %copy.8.start_ref, bf16[96,1024]{1,0:T(8,128)(2,1)S(1)} %copy-done, bf16[96,128]{1,0:T(8,128)(2,1)S(1)} %copy-done.1, bf16[96,128]{1,0:T(8,128)(2,1)S(1)} %copy-done.2), custom_call_target="tpu_custom_call" | custom-call | tf_op jit(solution)/shard_map/pallas_call | solution.py:472
  59.1 0.7 %copy.9 = f32[96,1024]{1,0:T(8,128)} copy(f32[96,1024]{1,0:T(8,128)S(1)} %get-tuple-element.8) | data formatting | bytes 786432
  59.8 0.6 copy.10
Async XLA Ops:
  1.3 0.9 %copy-start = (bf16[96,1024]{1,0:T(8,128)(2,1)S(1)}, bf16[96,1024]{1,0:T(8,128)(2,1)}, u32[]{:S(2)}) copy-start(bf16[96,1024]{1,0:T(8,128)(2,1)} %q_hbm.1) | copy-start | bytes 589828
  2.2 0.7 %copy-start.1 = (bf16[96,128]{1,0:T(8,128)(2,1)S(1)}, bf16[96,128]{1,0:T(8,128)(2,1)}, u32[]{:S(2)}) copy-start(bf16[96,128]{1,0:T(8,128)(2,1)} %k_hbm.1) | copy-start | bytes 73732
  2.9 0.7 %copy-start.2 = (bf16[96,128]{1,0:T(8,128)(2,1)S(1)}, bf16[96,128]{1,0:T(8,128)(2,1)}, u32[]{:S(2)}) copy-start(bf16[96,128]{1,0:T(8,128)(2,1)} %v_hbm.1) | copy-start | bytes 73732

commit v5 on v4

--- a/solution.py
+++ b/solution.py
@@ -229,29 +229,31 @@
         factor = jnp.concatenate([f[...], f[...]], axis=1)
         acc[query] = acc[query] * factor + jnp.dot(p[...], vals, preferred_element_type=jnp.float32)
 
-    def finish(k):
-        for half in range(2):
-            at = pl.ds(half * HALF, HALF)
-            total = acc[k, at, HD:2 * HD]
-            some = total > 0.0
-            safe = jnp.where(some, total, 1.0)
-            ob[k, half, 0:HALF, :] = (acc[k, at, 0:HD] / safe).astype(jnp.bfloat16)
-            log = jnp.where(some, peak[k, at, :] * SCALE + jnp.log(safe), MASKED)
-            hi = log.astype(jnp.bfloat16).astype(jnp.float32)
-            mid = (log - hi).astype(jnp.bfloat16).astype(jnp.float32)
-            low = log - hi - mid
-            packed = jnp.zeros((TOK, HD), jnp.float32)
-            for h in range(4):
-                for i, term in enumerate((hi, mid, low)):
-                    packed = jnp.where(lane == 3 * h + i, term[h * TOK:(h + 1) * TOK, :], packed)
-            packed = jnp.concatenate([packed, jnp.zeros((HD - TOK, HD), jnp.float32)], axis=0)
-            ob[k, half, HALF:OMSG, :] = packed.T[0:16, :].astype(jnp.bfloat16)
+    def finish(k, half):
+        at = pl.ds(half * HALF, HALF)
+        total = acc[k, at, HD:2 * HD]
+        safe = jnp.where(total > 0.0, total, 1.0)
+        ob[k, half, 0:HALF, :] = (acc[k, at, 0:HD] / safe).astype(jnp.bfloat16)
+        sums = jnp.ones((TOK, HD), jnp.float32)
+        tops = jnp.zeros((TOK, HD), jnp.float32)
+        for h in range(4):
+            mine = lax.div(lane, 3) == h
+            sums = jnp.where(mine, total[h * TOK:(h + 1) * TOK, :], sums)
+            tops = jnp.where(mine, peak[k, pl.ds(half * HALF + h * TOK, TOK), :], tops)
+        some = sums > 0.0
+        log = jnp.where(some, tops * SCALE + jnp.log(jnp.where(some, sums, 1.0)), MASKED)
+        hi = log.astype(jnp.bfloat16).astype(jnp.float32)
+        mid = (log - hi).astype(jnp.bfloat16).astype(jnp.float32)
+        turn_of = lax.rem(lane, 3)
+        packed = jnp.where(turn_of == 0, hi, jnp.where(turn_of == 1, mid, log - hi - mid))
+        packed = jnp.concatenate([packed, jnp.zeros((HD - TOK, HD), jnp.float32)], axis=0)
+        ob[k, half, HALF:OMSG, :] = packed.T[0:16, :].astype(jnp.bfloat16)
 
     def send_out(k):
-        finish(k)
-        for other in range(2):
-            if k or other:
-                start(o_copy, k, other)
+        for half in (1, 0):
+            finish(k, half)
+            if k or half:
+                start(o_copy, k, half)
 
     pl.semaphore_wait(barrier, 12 + 4 * c)
 
@@ -427,21 +429,20 @@
     gather(31, p_b, f_b)
     send_out(0)
 
-    for make, which in sent[2]:
+    for make, which in sent[2][:-1]:
         make(*which).wait_send()
     for core in range(2):
         @pl.when(c == core)
         def _():
             for make, which in sent[core]:
                 make(*which).wait_send()
-    for k in range(4):
-        for other in range(2):
-            if k or other:
-                o_wait(k, other)
 
     sub = lax.broadcasted_iota(jnp.int32, (16, HD), 0)
     totals = jnp.zeros((16, HD), jnp.float32)
     for other in range(2):
+        for k in range(4):
+            if k or other:
+                o_wait(k, other)
         half = c if other == 0 else 1 - c
         parts = [ob.at[0, 0] if k == 0 and other == 0 else rb.at[k, other] for k in range(4)]
         logs = [part_ref[HALF:OMSG, :].astype(jnp.float32) for part_ref in parts]
@@ -462,6 +463,8 @@
                 mixed += share * parts[k][h * TOK:(h + 1) * TOK, :].astype(jnp.float32)
             att_ref[:, pl.ds(pl.multiple_of((half * 4 + h) * HD, HD), HD)] = mixed
     lt_ref[...] = totals[0:8, 0:TOK]
+    make, which = sent[2][-1]
+    make(*which).wait_send()
 
 
 def local(queries, keys, values, block_start):

time: 60.7 us -> 60.7 us (level)
  no operation moved by 1% of the time
where the time goes in v5:
time: 60.7 us; the launch traced here: 60.5 us
  Pallas kernels  55.5 us (91%)
  local copies, waits for them, and re-layouts  3.73 us (6%)
  between operations  1.3 us (2%)
    pallas_call x1, Pallas kernels, local(): pl.pallas_call(kernel, out_shape=(jax.ShapeDtypeStruct((TOK, 8 * HD), f32...  55.5 us
    unnamed x8, local copies, waits for them, and re-layouts  3.73 us

profile of v5, /device:TPU:1, one launch (start us, length us, event | category | flops | bytes accessed | tf_op | source)
XLA Modules:
  0.0 60.5 jit_solution(16896908350928605525)
XLA Ops:
  1.3 0.0 copy-start
  1.3 0.9 %copy-done = bf16[96,1024]{1,0:T(8,128)(2,1)S(1)} copy-done((bf16[96,1024]{1,0:T(8,128)(2,1)S(1)}, bf16[96,1024]{1,0:T(8,128)(2,1)}, u32[]{:S(2)}) %copy-start) | copy-done | bytes 196632
  2.2 0.0 copy-start.1
  2.2 0.7 %copy-done.1 = bf16[96,128]{1,0:T(8,128)(2,1)S(1)} copy-done((bf16[96,128]{1,0:T(8,128)(2,1)S(1)}, bf16[96,128]{1,0:T(8,128)(2,1)}, u32[]{:S(2)}) %copy-start.1) | copy-done | bytes 24600
  2.9 0.0 copy-start.2
  2.9 0.7 %copy-done.2 = bf16[96,128]{1,0:T(8,128)(2,1)S(1)} copy-done((bf16[96,128]{1,0:T(8,128)(2,1)S(1)}, bf16[96,128]{1,0:T(8,128)(2,1)}, u32[]{:S(2)}) %copy-start.2) | copy-done | bytes 24600
  3.7 55.5 %shard_map.59 = (f32[96,1024]{1,0:T(8,128)S(1)}, f32[8,96]{1,0:T(8,128)S(1)}) custom-call(s32[1]{0:T(128)S(6)} %copy.8.start_ref, bf16[96,1024]{1,0:T(8,128)(2,1)S(1)} %copy-done, bf16[96,128]{1,0:T(8,128)(2,1)S(1)} %copy-done.1, bf16[96,128]{1,0:T(8,128)(2,1)S(1)} %copy-done.2), custom_call_target="tpu_custom_call" | custom-call | tf_op jit(solution)/shard_map/pallas_call | solution.py:475
  59.2 0.7 %copy.9 = f32[96,1024]{1,0:T(8,128)} copy(f32[96,1024]{1,0:T(8,128)S(1)} %get-tuple-element.8) | data formatting | bytes 786432
  59.9 0.6 copy.10
Async XLA Ops:
  1.3 0.9 %copy-start = (bf16[96,1024]{1,0:T(8,128)(2,1)S(1)}, bf16[96,1024]{1,0:T(8,128)(2,1)}, u32[]{:S(2)}) copy-start(bf16[96,1024]{1,0:T(8,128)(2,1)} %q_hbm.1) | copy-start | bytes 589828
  2.2 0.7 %copy-start.1 = (bf16[96,128]{1,0:T(8,128)(2,1)S(1)}, bf16[96,128]{1,0:T(8,128)(2,1)}, u32[]{:S(2)}) copy-start(bf16[96,128]{1,0:T(8,128)(2,1)} %k_hbm.1) | copy-start | bytes 73732
  2.9 0.7 %copy-start.2 = (bf16[96,128]{1,0:T(8,128)(2,1)S(1)}, bf16[96,128]{1,0:T(8,128)(2,1)}, u32[]{:S(2)}) copy-start(bf16[96,128]{1,0:T(8,128)(2,1)} %v_hbm.1) | copy-start | bytes 73732
